TPU v7x, 32 devices: a whole 2x2x4 slice. The times are simulated.
32 devices in a mesh: groups: 2 (over x), seq: 8 (over z, y), head: 2 (over core).
Axes of the slice: x: 2, y: 2, z: 4, core: 2. Of those that a mesh axis runs over, the one named last changes fastest.
Arguments:
- byte_ids: int32 [8192], P(('groups', 'seq')), parts along dimension 0, may hold values from 0 to 255
- embed_table: bfloat16 [256, 1024], P(None, 'head'), may hold values from -6 to 6
- gains: float32 [2, 1024], replicated, may hold values from 0.1 to 1.9
- conv_weight: bfloat16 [2, 3, 1024, 1024], P(None, None, None, 'head'), may hold values from -0.109375 to 0.109375
- conv_bias: float32 [2, 1024], P(None, 'head'), may hold values from -3 to 3
- qkv_weight: bfloat16 [3, 1024, 2048], P(None, None, 'head'), may hold values from -5 to 5
Outputs:
- context: bfloat16 [1024, 2048], P(('groups', 'seq'), 'head'), parts along dimension 0
There are 2 independent parts, one for each index of `groups`. A program takes and returns all parts, laid end to end along the dimension named above; an argument that names none is the same for every part. Nothing has to cross between parts.
All inputs are finite; a program needn't handle non-finite values.
Results may differ from a plain program's by a relative error of at most 0.0173.
The roundings to bfloat16 on the way count: a program that leaves them out, or rounds other values in their place, can miss the bound.
Values may be sent and summed in bfloat16 or wider, within the bound.
A program may use at most 128 MiB of HBM per device.

v0:
```python
import jax
import jax.numpy as jnp
from jax import lax
from jax.sharding import PartitionSpec as P

D = 1024
HEAD_SIZE = 64
LAYERS = 2
DILATION_FIRST = 1024
DILATION_SECOND = 2048
POOL = 8
epsilon = 1e-05


def activate(stream, gain_row, squares):
    rescale = lax.rsqrt(squares / D + epsilon)
    return jax.nn.gelu(stream * rescale[:, None] * gain_row[None, :], approximate=False).astype(
        jnp.bfloat16
    )


def slide(rows, amount):
    padding = jnp.zeros((abs(amount), rows.shape[1]), rows.dtype)
    if amount > 0:
        return jnp.concatenate([padding, rows[:-amount]], axis=0)
    return jnp.concatenate([rows[-amount:], padding], axis=0)


def attend(running, key_rows, value_rows, queries, query_pos, key_pos):
    row_max, totals, weighted = running
    heads_here = queries.shape[1]
    key_count = key_rows.shape[0]
    key_heads = key_rows.reshape(key_count, heads_here, HEAD_SIZE)
    value_heads = value_rows.reshape(key_count, heads_here, HEAD_SIZE)
    scores = jnp.einsum(
        "qhd,khd->hqk", queries, key_heads, preferred_element_type=jnp.float32
    ) * HEAD_SIZE ** (-0.5)
    visible = key_pos[None, None, :] <= query_pos[None, :, None]
    masked = jnp.where(visible, scores, -1e30)
    new_max = jnp.maximum(row_max, jnp.max(masked, axis=2))
    powers = jnp.where(visible, jnp.exp(masked - new_max[:, :, None]), 0.0)
    totals = jnp.sum(powers, axis=2)
    weighted = jnp.einsum("hqk,khd->hqd", powers, value_heads.astype(jnp.float32))
    return (new_max, totals, weighted)


def local(byte_ids, embed_table, gains, conv_weight, conv_bias, qkv_weight):
    row_count = byte_ids.shape[0]
    width_half = embed_table.shape[1]
    seq_count = lax.axis_size("seq")
    seq_place = lax.axis_index("seq")
    stride_cells = DILATION_FIRST // seq_count
    stride_pooled = stride_cells // POOL
    pooled_rows = row_count // POOL
    all_ids = lax.all_gather(byte_ids, "seq", axis=0, tiled=True)
    all_ids = all_ids.reshape(-1, seq_count, stride_cells)
    local_ids = lax.dynamic_slice_in_dim(all_ids, seq_place, 1, 1).reshape(row_count)
    vocab_ids = jnp.arange(embed_table.shape[0], dtype=jnp.int32)
    one_hot = (local_ids[:, None] == vocab_ids[None, :]).astype(jnp.bfloat16)
    stream = jnp.dot(one_hot, embed_table, preferred_element_type=jnp.float32)
    dilation_list = (DILATION_FIRST, DILATION_SECOND)
    for layer_index in range(LAYERS):
        local_step = dilation_list[layer_index] // DILATION_FIRST * stride_cells
        whole_rows = lax.all_gather(stream, "head", axis=1, tiled=True)
        active = activate(whole_rows, gains[layer_index], jnp.sum(whole_rows * whole_rows, axis=1))
        behind = slide(active, local_step)
        in_front = slide(active, -local_step)
        mixed = jnp.dot(behind, conv_weight[layer_index, 0], preferred_element_type=jnp.float32)
        mixed = mixed + jnp.dot(
            active, conv_weight[layer_index, 1], preferred_element_type=jnp.float32
        )
        mixed = mixed + jnp.dot(
            in_front, conv_weight[layer_index, 2], preferred_element_type=jnp.float32
        )
        stream = stream + mixed + conv_bias[layer_index][None, :]
    pooled = jnp.mean(stream.reshape(pooled_rows, POOL, width_half), axis=1).astype(jnp.bfloat16)
    pooled_full = lax.all_gather(pooled, "head", axis=1, tiled=True)
    heads_here = qkv_weight.shape[2] // HEAD_SIZE
    queries = jnp.dot(pooled_full, qkv_weight[0], preferred_element_type=jnp.float32).astype(
        jnp.bfloat16
    )
    queries = queries.reshape(pooled_rows, heads_here, HEAD_SIZE)
    period = DILATION_FIRST // POOL

    def key_places(offset, count):
        rows_here = offset + jnp.arange(count, dtype=jnp.int32)
        source = rows_here // pooled_rows
        inner = rows_here % pooled_rows
        return inner // stride_pooled * period + source * stride_pooled + inner % stride_pooled

    query_pos = key_places(seq_place * pooled_rows, pooled_rows)
    start_state = (
        jnp.full((heads_here, pooled_rows), -1e30, jnp.float32),
        jnp.zeros((heads_here, pooled_rows), jnp.float32),
        jnp.zeros((heads_here, pooled_rows, HEAD_SIZE), jnp.float32),
    )
    key_rows = jnp.dot(pooled_full, qkv_weight[1], preferred_element_type=jnp.float32).astype(
        jnp.bfloat16
    )
    value_rows = jnp.dot(pooled_full, qkv_weight[2], preferred_element_type=jnp.float32).astype(
        jnp.bfloat16
    )
    pieces = (
        lax.all_gather(key_rows, "seq", axis=0, tiled=True),
        lax.all_gather(value_rows, "seq", axis=0, tiled=True),
    )
    row_max, totals, weighted = attend(
        start_state,
        pieces[0],
        pieces[1],
        queries,
        query_pos,
        key_places(jnp.int32(0), pieces[0].shape[0]),
    )
    out_width = heads_here * HEAD_SIZE
    context = (weighted / totals[:, :, None]).transpose(1, 0, 2).reshape(pooled_rows, out_width)
    context = context.astype(jnp.bfloat16)
    block_count = pooled_rows // stride_pooled
    fan_count = seq_count // block_count
    target = seq_place * stride_pooled // pooled_rows
    picked_dilation = jnp.arange(fan_count, dtype=jnp.int32) == target
    sectioned = jnp.where(
        picked_dilation[None, :, None, None],
        context.reshape(block_count, 1, stride_pooled, out_width),
        jnp.zeros((), jnp.bfloat16),
    )
    sectioned = sectioned.reshape(seq_count * stride_pooled, out_width)
    arrived = lax.all_to_all(sectioned, "seq", split_axis=0, concat_axis=0, tiled=True)
    arrived = arrived.reshape(seq_count, stride_pooled, out_width)
    context = lax.dynamic_slice_in_dim(arrived, seq_place % fan_count * block_count, block_count, 0)
    context = context.reshape(pooled_rows, out_width)
    return context


def solution(mesh):
    placed = (
        P(("groups", "seq")),
        P(None, "head"),
        P(),
        P(None, None, None, "head"),
        P(None, "head"),
        P(None, None, "head"),
    )
    return jax.shard_map(
        local, mesh=mesh, in_specs=placed, out_specs=P(("groups", "seq"), "head"), check_vma=False
    )
```

profile of v0, /device:TPU:0, one launch (start us, length us, event | category | flops | bytes accessed | tf_op | source)
XLA Modules:
  0.0 191.9 jit_solution(12096868458623567444)
XLA Ops:
  6.6 28.1 %all-gather = s32[8,1,512]{2,1,0:T(1,128)S(1)} all-gather(s32[1,1,512]{2,1,0:T(1,128)} %bitcast.72), channel_id=1, replica_groups=mesh['groups'=2,'seq'=8,'head'=2] {'seq'}, dimensions={0}, use_global_device_ids=true | all-gather | bytes 18432 | tf_op jit(solution)/shard_map/all_gather | solution.py:55
  34.6 1.3 fusion.73
  36.0 0.0 all-gather.6.cloned.1.call-update
  36.0 0.0 all-gather.8.cloned.1.call-start
  36.0 0.0 copy-done.6
  36.1 9.9 %all-gather.6.cloned.1.call-done = f32[512,1024]{1,0:T(8,128)} async-done(((f32[512,512]{1,0:T(8,128)}), f32[512,1024]{1,0:T(8,128)}) %all-gather.6.cloned.1.call-update) | async-done | bytes 2097168 | tf_op jit(solution)/shard_map/all_gather | solution.py:64
  46.0 2.0 %multiply_reduce_fusion.1 = f32[512]{0:T(512)S(1)} fusion(f32[512,1024]{1,0:T(8,128)} %all-gather.6.cloned.1.call-done), kind=kLoop, calls=%fused_computation.48 | loop fusion | flops 1048064 | bytes 2099200 | tf_op jit(solution)/shard_map/reduce_sum | solution.py:65
  48.0 0.3 copy-done.2
  48.2 5.1 %fusion.2 = bf16[512,1024]{1,0:T(8,128)(2,1)S(1)} fusion(f32[512,1024]{1,0:T(8,128)S(1)} %copy-done.2, f32[1024]{0:T(1024)S(1)} %bitcast.68, f32[512]{0:T(512)S(1)} %add_rsqrt_fusion.1), kind=kLoop, calls=%fused_computation.4 | loop fusion | flops 35127296 | bytes 3151872 | tf_op jit(solution)/shard_map/convert_element_type | solution.py:17
  53.3 0.2 fusion.99
  53.5 0.0 copy-done.5
  53.5 0.7 fusion.56
  54.2 0.7 convolution_add_fusion.3
  54.9 0.5 copy-done.1
  55.4 1.7 fusion.34
  57.1 0.0 all-gather.8.cloned.1.call-update
  57.1 0.0 all-gather.10.cloned.1.call-start
  57.2 11.9 %all-gather.8.cloned.1.call-done = f32[512,1024]{1,0:T(8,128)} async-done(((f32[512,512]{1,0:T(8,128)}), f32[512,1024]{1,0:T(8,128)}) %all-gather.8.cloned.1.call-update) | async-done | bytes 2097168 | tf_op jit(solution)/shard_map/all_gather | solution.py:64
  69.1 2.0 %multiply_reduce_fusion = f32[512]{0:T(512)S(1)} fusion(f32[512,1024]{1,0:T(8,128)} %all-gather.8.cloned.1.call-done), kind=kLoop, calls=%fused_computation.33 | loop fusion | flops 1048064 | bytes 2099200 | tf_op jit(solution)/shard_map/reduce_sum | solution.py:65
  71.0 0.3 copy-done.3
  71.3 5.1 %fusion.5 = bf16[512,1024]{1,0:T(8,128)(2,1)S(1)} fusion(f32[512,1024]{1,0:T(8,128)S(1)} %copy-done.3, f32[1024]{0:T(1024)S(1)} %bitcast.67, f32[512]{0:T(512)S(1)} %add_rsqrt_fusion), kind=kLoop, calls=%fused_computation.7 | loop fusion | flops 35127296 | bytes 3151872 | tf_op jit(solution)/shard_map/convert_element_type | solution.py:17
  76.3 0.1 fusion.98
  76.4 1.9 %fusion.52 = f32[512,512]{1,0:T(8,128)S(1)} fusion(bf16[2,3,1024,512]{3,2,1,0:T(8,128)(2,1)} %param.9, bf16[256,1024]{1,0:T(8,128)(2,1)S(1)} %get-tuple-element.6), kind=kOutput, calls=%fused_computation.74 | convolution fusion | flops 536870912 | bytes 2621440 | tf_op jit(solution)/shard_map/dot_general | solution.py:68
  78.4 2.0 %convolution_add_fusion.1 = f32[512,512]{1,0:T(8,128)S(1)} fusion(f32[512,512]{1,0:T(8,128)S(1)} %fusion.52, bf16[512,1024]{1,0:T(8,128)(2,1)S(1)} %fusion.5, bf16[2,3,1024,512]{3,2,1,0:T(8,128)(2,1)} %param.9), kind=kOutput, calls=%fused_computation.58 | convolution fusion | flops 537133056 | bytes 4194304 | tf_op jit(solution)/shard_map/dot_general | solution.py:69
  80.4 2.2 %fusion.37 = f32[64,512]{1,0:T(8,128)S(1)} fusion(f32[512,512]{1,0:T(8,128)S(1)} %copy-done.4, f32[512,512]{1,0:T(8,128)S(1)} %convolution_add_fusion.1, bf16[2,3,1024,512]{3,2,1,0:T(8,128)(2,1)} %param.9, bf16[256,1024]{1,0:T(8,128)(2,1)S(1)} %get-tuple-element.5, f32[512]{0:T(512)S(1)} %bitcast.73), kind=kOutput, calls=%fused_computation.65 | convolution fusion | flops 537886720 | bytes 3803136 | tf_op jit(solution)/shard_map/dot_general | solution.py:72
  82.6 1.9 all_gather.21
  84.5 2.7 %fusion.42 = bf16[64,1024]{1,0:T(8,128)(2,1)} fusion(bf16[64,1024]{1,0:T(8,128)(2,1)S(1)} %all_gather.21, bf16[3,1024,1024]{2,1,0:T(8,128)(2,1)} %param.11), kind=kOutput, calls=%fused_computation.68 | convolution fusion | flops 134283264 | bytes 2359296 | tf_op jit(solution)/shard_map/dot_general | solution.py:97
  87.2 0.0 all-gather.10.cloned.1.call-update
  87.3 0.2 all-gather.12.cloned.1.call-start
  87.5 2.7 %fusion.45 = bf16[64,1024]{1,0:T(8,128)(2,1)} fusion(bf16[64,1024]{1,0:T(8,128)(2,1)S(1)} %all_gather.21, bf16[3,1024,1024]{2,1,0:T(8,128)(2,1)} %param.11), kind=kOutput, calls=%fused_computation.69 | convolution fusion | flops 134283264 | bytes 2359296 | tf_op jit(solution)/shard_map/dot_general | solution.py:100
  90.2 0.0 all-gather.12.cloned.1.call-update
  90.3 0.1 broadcast_in_dim.56
  90.4 0.1 broadcast_compare_fusion
  90.5 2.1 %fusion.39 = bf16[64,1024]{1,0:T(8,128)(2,1)S(1)} fusion(bf16[64,1024]{1,0:T(8,128)(2,1)S(1)} %all_gather.21, bf16[3,1024,1024]{2,1,0:T(8,128)(2,1)} %param.11), kind=kOutput, calls=%fused_computation.67 | convolution fusion | flops 134283264 | bytes 2359296 | tf_op jit(solution)/shard_map/dot_general | solution.py:79
  92.6 0.9 reshape.205
  93.5 35.3 %all-gather.10.cloned.1.call-done = bf16[512,1024]{1,0:T(8,128)(2,1)} async-done(((bf16[64,1024]{1,0:T(8,128)(2,1)}), bf16[512,1024]{1,0:T(8,128)(2,1)}) %all-gather.10.cloned.1.call-update) | async-done | bytes 1048592 | tf_op jit(solution)/shard_map/all_gather | solution.py:104
  128.7 1.5 copy.14
  130.2 1.5 fusion.29
  131.7 0.7 fusion.30
  132.4 37.2 %all-gather.12.cloned.1.call-done = bf16[512,1024]{1,0:T(8,128)(2,1)} async-done(((bf16[64,1024]{1,0:T(8,128)(2,1)}), bf16[512,1024]{1,0:T(8,128)(2,1)}) %all-gather.12.cloned.1.call-update) | async-done | bytes 1048592 | tf_op jit(solution)/shard_map/all_gather | solution.py:105
  169.7 1.5 copy.16
  171.2 0.7 fusion.49
  171.9 0.2 copy.17
  172.1 0.2 convert_element_type.37
  172.3 0.8 bitcast_select_fusion
  173.0 3.4 %all-to-all-start = ((bf16[8,16,1024]{2,1,0:T(8,128)(2,1)}), bf16[8,16,1024]{2,1,0:T(8,128)(2,1)S(1)}, u32[]{:S(2)}, u32[]{:S(2)}) async-start(bf16[8,16,1024]{2,1,0:T(8,128)(2,1)} %bitcast_select_fusion), calls=%async_computation | async-start | bytes 524288 | tf_op jit(solution)/shard_map/all_to_all | solution.py:128
  176.5 8.3 %all-to-all-done = bf16[8,16,1024]{2,1,0:T(8,128)(2,1)S(1)} async-done(((bf16[8,16,1024]{2,1,0:T(8,128)(2,1)}), bf16[8,16,1024]{2,1,0:T(8,128)(2,1)S(1)}, u32[]{:S(2)}, u32[]{:S(2)}) %all-to-all-start) | async-done | bytes 262176 | tf_op jit(solution)/shard_map/all_to_all | solution.py:128
  184.7 0.7 constant_dynamic-slice_fusion
  (23 shorter events, 0.1 us)
Async XLA Ops:
  6.5 28.1 %copy-start = (bf16[256,512]{1,0:T(8,128)(2,1)S(1)}, bf16[256,512]{1,0:T(8,128)(2,1)}, u32[]{:S(2)}) copy-start(bf16[256,512]{1,0:T(8,128)(2,1)} %param.7) | copy-start | bytes 786436
  6.5 29.5 %copy-start.7 = (f32[2,512]{1,0:T(2,128)S(1)}, f32[2,512]{1,0:T(2,128)}, u32[]{:S(2)}) copy-start(f32[2,512]{1,0:T(2,128)} %param.10) | copy-start | bytes 12292
  6.5 29.5 %copy-start.6 = (f32[2,1024]{1,0:T(2,128)S(1)}, f32[2,1024]{1,0:T(2,128)}, u32[]{:S(2)}) copy-start(f32[2,1024]{1,0:T(2,128)} %param.8) | copy-start | bytes 24580
  6.5 39.5 %all-gather.6.cloned.1.call-start = ((), (), s32[]{:S(2)}) async-start(), calls=%async_computation.1 | async-start | bytes 3145728 | tf_op jit(solution)/shard_map/all_gather | solution.py:64
  36.0 33.1 %all-gather.8.cloned.1.call-start = ((), (), s32[]{:S(2)}) async-start(), calls=%async_computation.2 | async-start | bytes 3145728 | tf_op jit(solution)/shard_map/all_gather | solution.py:64
  46.0 2.2 %copy-start.2 = (f32[512,1024]{1,0:T(8,128)S(1)}, f32[512,1024]{1,0:T(8,128)}, u32[]{:S(2)}) copy-start(f32[512,1024]{1,0:T(8,128)} %all-gather.6.cloned.1.call-done) | copy-start | bytes 6291460
  48.2 5.3 %copy-start.5 = (bf16[2,3,1024,512]{3,2,1,0:T(8,128)(2,1)S(1)}, bf16[2,3,1024,512]{3,2,1,0:T(8,128)(2,1)}, u32[]{:S(2)}) copy-start(bf16[2,3,1024,512]{3,2,1,0:T(8,128)(2,1)} %param.9) | copy-start | bytes 18874372
  54.2 1.2 copy-start.1
  57.1 71.6 %all-gather.10.cloned.1.call-start = ((), (), s32[]{:S(2)}) async-start(), calls=%async_computation.3 | async-start | bytes 1179648 | tf_op jit(solution)/shard_map/all_gather | solution.py:104
  69.1 2.2 %copy-start.3 = (f32[512,1024]{1,0:T(8,128)S(1)}, f32[512,1024]{1,0:T(8,128)}, u32[]{:S(2)}) copy-start(f32[512,1024]{1,0:T(8,128)} %all-gather.8.cloned.1.call-done) | copy-start | bytes 6291460
  78.4 2.0 %copy-start.4 = (f32[512,512]{1,0:T(8,128)S(1)}, f32[512,512]{1,0:T(8,128)}, u32[]{:S(2)}) copy-start(f32[512,512]{1,0:T(8,128)} %fusion.34) | copy-start | bytes 3145732
  87.3 82.4 %all-gather.12.cloned.1.call-start = ((), (), s32[]{:S(2)}) async-start(), calls=%async_computation.4 | async-start | bytes 1179648 | tf_op jit(solution)/shard_map/all_gather | solution.py:105
  173.0 11.7 %all-to-all-start = ((bf16[8,16,1024]{2,1,0:T(8,128)(2,1)}), bf16[8,16,1024]{2,1,0:T(8,128)(2,1)S(1)}, u32[]{:S(2)}, u32[]{:S(2)}) async-start(bf16[8,16,1024]{2,1,0:T(8,128)(2,1)} %bitcast_select_fusion), calls=%async_computation | async-start | bytes 524288 | tf_op jit(solution)/shard_map/all_to_all | solution.py:128
Sparse Core Ops, SparseCore 0:
  36.1 9.8 all-gather.5
  57.3 11.7 all-gather.7
  87.4 41.3 all-gather.9
  130.7 38.8 all-gather.11
where the time goes:
time: 192 us
  waiting for transfers between devices  103 us (54%)
  blocking collectives  30 us (16%)
  matrix products  20.3 us (11%)
  other arithmetic  15.7 us (8%)
  between operations  13.4 us (7%)
  local copies, waits for them, and re-layouts  6.31 us (3%)
  starting transfers between devices  3.72 us (2%)
    all_gather x1, waiting for transfers between devices, local(): lax.all_gather(value_rows, 'seq', axis=0, tiled=True)  37.2 us
    all_gather x1, waiting for transfers between devices, local(): lax.all_gather(key_rows, 'seq', axis=0, tiled=True)  35.3 us
    all_gather x1, blocking collectives, local(): all_ids = lax.all_gather(byte_ids, 'seq', axis=0, tiled=True)  28.1 us
    all_gather x2, waiting for transfers between devices, local(): whole_rows = lax.all_gather(stream, 'head', axis=1, tiled=True)  21.8 us
    convert_element_type x2, other arithmetic, activate(): jax.nn.gelu(stream * rescale[:, None] * gain_row[None, :], approximate=Fa...  10.1 us
    all_to_all x1, waiting for transfers between devices, local(): lax.all_to_all(sectioned, 'seq', split_axis=0, concat_axis=0, tiled=True)  8.27 us
    reduce_sum x2, other arithmetic, local(): jnp.sum(whole_rows * whole_rows, axis=1)  3.9 us
    dot_general x2, matrix products, local(): jnp.dot(in_front, conv_weight[layer_index, 2], preferred_element_type=jnp...  3.87 us
  transfers between devices with their start and end apart: 5, of which 5 were waited for; matrix products, arithmetic and copies ran while one was open for 5% of the time, Pallas kernels for 0%

commit v1 on v0

--- a/solution.py
+++ b/solution.py
@@ -1,3 +1,4 @@
+import functools
 import jax
 import jax.numpy as jnp
 from jax import lax
@@ -10,6 +11,41 @@
 DILATION_SECOND = 2048
 POOL = 8
 epsilon = 1e-05
+
+
+def _pass_outputs(sample, axis_tag):
+    runs = []
+    piece_now, ready, all_values = (
+        lax.axis_size(axis_tag),
+        lax.axis_index(axis_tag),
+        sample.shape[0],
+    )
+    for idx, s in enumerate(sample.shape):
+        runs.append(s * piece_now if idx == 0 else s)
+    carry_in = v_next = sample
+    f_next = lax.dynamic_update_slice_in_dim(
+        jnp.zeros(runs, sample.dtype), sample, ready * all_values, axis=0
+    )
+    for d in range(1, piece_now // 2 + 1):
+        blocks_here = []
+        for idx in range(piece_now):
+            blocks_here.append((idx, (idx + 1) % piece_now))
+        carry_in = lax.ppermute(carry_in, axis_name=axis_tag, perm=blocks_here)
+        f_next = lax.dynamic_update_slice_in_dim(
+            f_next, carry_in, (ready - d) % piece_now * all_values, axis=0
+        )
+        if 2 * d < piece_now:
+            entries = []
+            for idx in range(piece_now):
+                entries.append((idx, (idx - 1) % piece_now))
+            v_next = lax.ppermute(v_next, axis_tag, entries)
+            f_next = lax.dynamic_update_slice_in_dim(
+                f_next, v_next, (ready + d) % piece_now * all_values, axis=0
+            )
+    return f_next
+
+
+measure_the_shifts_all = functools.partial(_pass_outputs, axis_tag="seq")
 
 
 def activate(stream, gain_row, squares):
@@ -101,7 +137,7 @@
         jnp.bfloat16
     )
     pieces = (
-        lax.all_gather(key_rows, "seq", axis=0, tiled=True),
+        measure_the_shifts_all(key_rows),
         lax.all_gather(value_rows, "seq", axis=0, tiled=True),
     )
     row_max, totals, weighted = attend(

time: 192 us -> 161 us (0.84)
  waiting for transfers between devices: 103 us -> 42.1 us
  starting transfers between devices: 3.72 us -> 20.5 us
  local copies, waits for them, and re-layouts: 6.31 us -> 18.8 us
    all_gather x1, waiting for transfers between devices: 37.2 us -> 0.02 us  [local(): lax.all_gather(value_rows, 'seq', axis=0, tiled=True)]
    all_gather x1 -> x0, waiting for transfers between devices: 35.3 us -> none  [local(): lax.all_gather(key_rows, 'seq', axis=0, tiled=True)]
    ppermute x0 -> x7, starting transfers between devices: none -> 14.4 us  [the longest x3 10.9 us: _pass_outputs(): v_next = lax.ppermute(v_next, axis_tag, entries)]
    dynamic_update_slice x0 -> x8, local copies, waits for them, and re-layouts: none -> 12.5 us  [the longest x4 6.07 us: _pass_outputs(): lax.dynamic_update_slice_in_dim(f_next, carry_in, (ready - d) % piece_now...]
    ppermute x0 -> x7, waiting for transfers between devices: none -> 12 us  [the longest x4 12 us: _pass_outputs(): carry_in = lax.ppermute(carry_in, axis_name=axis_tag, perm=blocks_here)]
    all_to_all x1, starting transfers between devices: 3.41 us -> 6 us  [local(): lax.all_to_all(sectioned, 'seq', split_axis=0, concat_axis=0, tiled=True)]
  transfers between devices with their start and end apart: 5 -> 11, of which waited for: 5 -> 6; matrix products, arithmetic and copies ran while one was open for 5% -> 13% of each run, Pallas kernels for 0% -> 0%
where the time goes in v1:
time: 161 us; the launch traced here: 160 us
  waiting for transfers between devices  42.1 us (26%)
  blocking collectives  30 us (19%)
  starting transfers between devices  20.5 us (13%)
  matrix products  19.6 us (12%)
  local copies, waits for them, and re-layouts  18.8 us (12%)
  other arithmetic  15.6 us (10%)
  between operations  13.5 us (8%)
    all_gather x1, blocking collectives, local(): all_ids = lax.all_gather(byte_ids, 'seq', axis=0, tiled=True)  28.1 us
    all_gather x2, waiting for transfers between devices, local(): whole_rows = lax.all_gather(stream, 'head', axis=1, tiled=True)  21.8 us
    ppermute x4, waiting for transfers between devices, _pass_outputs(): carry_in = lax.ppermute(carry_in, axis_name=axis_tag, perm=blocks_here)  12 us
    ppermute x3, starting transfers between devices, _pass_outputs(): v_next = lax.ppermute(v_next, axis_tag, entries)  10.9 us
    convert_element_type x2, other arithmetic, activate(): jax.nn.gelu(stream * rescale[:, None] * gain_row[None, :], approximate=Fa...  10.1 us
    all_to_all x1, waiting for transfers between devices, local(): lax.all_to_all(sectioned, 'seq', split_axis=0, concat_axis=0, tiled=True)  8.22 us
    dynamic_update_slice x4, local copies, waits for them, and re-layouts, _pass_outputs(): lax.dynamic_update_slice_in_dim(f_next, carry_in, (ready - d) % piece_now...  6.07 us
    all_to_all x1, starting transfers between devices, local(): lax.all_to_all(sectioned, 'seq', split_axis=0, concat_axis=0, tiled=True)  6 us
  transfers between devices with their start and end apart: 11, of which 6 were waited for; matrix products, arithmetic and copies ran while one was open for 13% of the time, Pallas kernels for 0%

profile of v1, /device:TPU:0, one launch (start us, length us, event | category | flops | bytes accessed | tf_op | source)
XLA Modules:
  0.0 160.0 jit_solution(13024990545040487658)
XLA Ops:
  6.6 28.1 %all-gather = s32[8,1,512]{2,1,0:T(1,128)S(1)} all-gather(s32[1,1,512]{2,1,0:T(1,128)} %bitcast.72), channel_id=1, replica_groups=mesh['groups'=2,'seq'=8,'head'=2] {'seq'}, dimensions={0}, use_global_device_ids=true | all-gather | bytes 18432 | tf_op jit(solution)/shard_map/all_gather | solution.py:91
  34.6 1.3 fusion.73
  36.1 9.9 %all-gather.5.cloned.1.call-done = f32[512,1024]{1,0:T(8,128)} async-done(((f32[512,512]{1,0:T(8,128)}), f32[512,1024]{1,0:T(8,128)}) %all-gather.5.cloned.1.call-update) | async-done | bytes 2097168 | tf_op jit(solution)/shard_map/all_gather | solution.py:100
  46.0 2.0 %multiply_reduce_fusion.1 = f32[512]{0:T(512)S(1)} fusion(f32[512,1024]{1,0:T(8,128)} %all-gather.5.cloned.1.call-done), kind=kLoop, calls=%fused_computation.48 | loop fusion | flops 1048064 | bytes 2099200 | tf_op jit(solution)/shard_map/reduce_sum | solution.py:101
  48.0 0.3 copy-done.2
  48.2 5.1 %fusion.2 = bf16[512,1024]{1,0:T(8,128)(2,1)S(1)} fusion(f32[512,1024]{1,0:T(8,128)S(1)} %copy-done.2, f32[1024]{0:T(1024)S(1)} %bitcast.68, f32[512]{0:T(512)S(1)} %add_rsqrt_fusion.1), kind=kLoop, calls=%fused_computation.4 | loop fusion | flops 35127296 | bytes 3151872 | tf_op jit(solution)/shard_map/convert_element_type | solution.py:53
  53.3 0.2 fusion.99
  53.5 0.7 fusion.56
  54.2 0.7 convolution_add_fusion.3
  54.9 0.5 copy-done.1
  55.4 1.7 %fusion.34 = f32[512,512]{1,0:T(8,128)} fusion(f32[512,512]{1,0:T(8,128)S(1)} %copy-done.1, f32[512,512]{1,0:T(8,128)S(1)} %convolution_add_fusion.3, bf16[2,3,1024,512]{3,2,1,0:T(8,128)(2,1)S(1)} %copy-done.5, bf16[384,1024]{1,0:T(8,128)(2,1)S(1)} %get-tuple-element.7, f32[512]{0:T(512)S(1)} %bitcast.71), kind=kOutput, calls=%fused_computation.62 | convolution fusion | flops 537657344 | bytes 4982784 | tf_op jit(solution)/shard_map/dot_general | solution.py:108
  57.2 11.9 %all-gather.7.cloned.1.call-done = f32[512,1024]{1,0:T(8,128)} async-done(((f32[512,512]{1,0:T(8,128)}), f32[512,1024]{1,0:T(8,128)}) %all-gather.7.cloned.1.call-update) | async-done | bytes 2097168 | tf_op jit(solution)/shard_map/all_gather | solution.py:100
  69.0 2.0 %multiply_reduce_fusion = f32[512]{0:T(512)S(1)} fusion(f32[512,1024]{1,0:T(8,128)} %all-gather.7.cloned.1.call-done), kind=kLoop, calls=%fused_computation.33 | loop fusion | flops 1048064 | bytes 2099200 | tf_op jit(solution)/shard_map/reduce_sum | solution.py:101
  71.0 0.3 copy-done.3
  71.3 5.1 %fusion.5 = bf16[512,1024]{1,0:T(8,128)(2,1)S(1)} fusion(f32[512,1024]{1,0:T(8,128)S(1)} %copy-done.3, f32[1024]{0:T(1024)S(1)} %bitcast.67, f32[512]{0:T(512)S(1)} %add_rsqrt_fusion), kind=kLoop, calls=%fused_computation.7 | loop fusion | flops 35127296 | bytes 3151872 | tf_op jit(solution)/shard_map/convert_element_type | solution.py:53
  76.4 1.9 %fusion.52 = f32[512,512]{1,0:T(8,128)S(1)} fusion(bf16[2,3,1024,512]{3,2,1,0:T(8,128)(2,1)} %param.9, bf16[256,1024]{1,0:T(8,128)(2,1)S(1)} %get-tuple-element.6), kind=kOutput, calls=%fused_computation.74 | convolution fusion | flops 536870912 | bytes 2621440 | tf_op jit(solution)/shard_map/dot_general | solution.py:104
  78.4 2.0 %convolution_add_fusion.1 = f32[512,512]{1,0:T(8,128)S(1)} fusion(f32[512,512]{1,0:T(8,128)S(1)} %fusion.52, bf16[512,1024]{1,0:T(8,128)(2,1)S(1)} %fusion.5, bf16[2,3,1024,512]{3,2,1,0:T(8,128)(2,1)} %param.9), kind=kOutput, calls=%fused_computation.58 | convolution fusion | flops 537133056 | bytes 4194304 | tf_op jit(solution)/shard_map/dot_general | solution.py:105
  80.4 2.2 %fusion.37 = f32[64,512]{1,0:T(8,128)S(1)} fusion(f32[512,512]{1,0:T(8,128)S(1)} %copy-done.4, f32[512,512]{1,0:T(8,128)S(1)} %convolution_add_fusion.1, bf16[2,3,1024,512]{3,2,1,0:T(8,128)(2,1)} %param.9, bf16[256,1024]{1,0:T(8,128)(2,1)S(1)} %get-tuple-element.5, f32[512]{0:T(512)S(1)} %bitcast.73), kind=kOutput, calls=%fused_computation.65 | convolution fusion | flops 537886720 | bytes 3803136 | tf_op jit(solution)/shard_map/dot_general | solution.py:108
  82.6 1.9 %all_gather.18 = bf16[64,1024]{1,0:T(8,128)(2,1)S(1)} all-gather(bf16[64,512]{1,0:T(8,128)(2,1)S(1)} %multiply_convert_fusion), channel_id=1, replica_groups=mesh['groups'=2,'seq'=8,'head'=2] {'head'}, dimensions={1}, use_global_device_ids=true | all-gather | bytes 196608 | tf_op jit(solution)/shard_map/all_gather | solution.py:113
  84.5 2.7 %fusion.45 = bf16[64,1024]{1,0:T(8,128)(2,1)} fusion(bf16[64,1024]{1,0:T(8,128)(2,1)S(1)} %all_gather.18, bf16[3,1024,1024]{2,1,0:T(8,128)(2,1)} %param.11), kind=kOutput, calls=%fused_computation.69 | convolution fusion | flops 134283264 | bytes 2359296 | tf_op jit(solution)/shard_map/dot_general | solution.py:136
  87.3 2.1 %fusion.42 = bf16[64,1024]{1,0:T(8,128)(2,1)S(1)} fusion(bf16[64,1024]{1,0:T(8,128)(2,1)S(1)} %all_gather.18, bf16[3,1024,1024]{2,1,0:T(8,128)(2,1)} %param.11), kind=kOutput, calls=%fused_computation.68 | convolution fusion | flops 134283264 | bytes 2359296 | tf_op jit(solution)/shard_map/dot_general | solution.py:133
  89.3 1.8 %collective-permute-start = (bf16[64,1024]{1,0:T(8,128)(2,1)S(1)}, bf16[64,1024]{1,0:T(8,128)(2,1)S(1)}, u32[]{:S(2)}, u32[]{:S(2)}) collective-permute-start(bf16[64,1024]{1,0:T(8,128)(2,1)S(1)} %fusion.42), channel_id=1, source_target_pairs={{0,2},{2,4},{4,6},{6,8},{8,10},{10,12},{12,14},{14,0},{1,3},{3,5},... | collective-permute-start | bytes 393224 | tf_op jit(solution)/shard_map/ppermute | solution.py:33
  91.1 3.0 %collective-permute-start.1 = (bf16[64,1024]{1,0:T(8,128)(2,1)S(1)}, bf16[64,1024]{1,0:T(8,128)(2,1)S(1)}, u32[]{:S(2)}, u32[]{:S(2)}) collective-permute-start(bf16[64,1024]{1,0:T(8,128)(2,1)S(1)} %fusion.42), channel_id=1, source_target_pairs={{0,14},{2,0},{4,2},{6,4},{8,6},{10,8},{12,10},{14,12},{1,15},{3,1}... | collective-permute-start | bytes 393224 | tf_op jit(solution)/shard_map/ppermute | solution.py:41
  94.2 3.8 %collective-permute-done = bf16[64,1024]{1,0:T(8,128)(2,1)S(1)} collective-permute-done((bf16[64,1024]{1,0:T(8,128)(2,1)S(1)}, bf16[64,1024]{1,0:T(8,128)(2,1)S(1)}, u32[]{:S(2)}, u32[]{:S(2)}) %collective-permute-start) | collective-permute-done | bytes 131104 | tf_op jit(solution)/shard_map/ppermute | solution.py:33
  98.0 1.7 %collective-permute-start.2 = (bf16[64,1024]{1,0:T(8,128)(2,1)S(1)}, bf16[64,1024]{1,0:T(8,128)(2,1)S(1)}, u32[]{:S(2)}, u32[]{:S(2)}) collective-permute-start(bf16[64,1024]{1,0:T(8,128)(2,1)S(1)} %collective-permute-done), channel_id=1, source_target_pairs={{0,2},{2,4},{4,6},{6,8},{8,10},{10,12},{12,14},{14,0},{1,3},{3,5},... | collective-permute-start | bytes 393224 | tf_op jit(solution)/shard_map/ppermute | solution.py:33
  99.8 3.1 %collective-permute-start.3 = (bf16[64,1024]{1,0:T(8,128)(2,1)S(1)}, bf16[64,1024]{1,0:T(8,128)(2,1)S(1)}, u32[]{:S(2)}, u32[]{:S(2)}) collective-permute-start(bf16[64,1024]{1,0:T(8,128)(2,1)S(1)} %collective-permute-done.1), channel_id=1, source_target_pairs={{0,14},{2,0},{4,2},{6,4},{8,6},{10,8},{12,10},{14,12},{1,15},{3,1}... | collective-permute-start | bytes 393224 | tf_op jit(solution)/shard_map/ppermute | solution.py:41
  102.9 5.3 %collective-permute-done.2 = bf16[64,1024]{1,0:T(8,128)(2,1)S(1)} collective-permute-done((bf16[64,1024]{1,0:T(8,128)(2,1)S(1)}, bf16[64,1024]{1,0:T(8,128)(2,1)S(1)}, u32[]{:S(2)}, u32[]{:S(2)}) %collective-permute-start.2) | collective-permute-done | bytes 131104 | tf_op jit(solution)/shard_map/ppermute | solution.py:33
  108.3 4.8 %collective-permute-start.5 = (bf16[64,1024]{1,0:T(8,128)(2,1)S(1)}, bf16[64,1024]{1,0:T(8,128)(2,1)S(1)}, u32[]{:S(2)}, u32[]{:S(2)}) collective-permute-start(bf16[64,1024]{1,0:T(8,128)(2,1)S(1)} %collective-permute-done.3), channel_id=1, source_target_pairs={{0,14},{2,0},{4,2},{6,4},{8,6},{10,8},{12,10},{14,12},{1,15},{3,1}... | collective-permute-start | bytes 393224 | tf_op jit(solution)/shard_map/ppermute | solution.py:41
  113.1 2.9 %collective-permute-done.4 = bf16[64,1024]{1,0:T(8,128)(2,1)S(1)} collective-permute-done((bf16[64,1024]{1,0:T(8,128)(2,1)S(1)}, bf16[64,1024]{1,0:T(8,128)(2,1)S(1)}, u32[]{:S(2)}, u32[]{:S(2)}) %collective-permute-start.4) | collective-permute-done | bytes 131104 | tf_op jit(solution)/shard_map/ppermute | solution.py:33
  116.0 2.1 %fusion.39 = bf16[64,1024]{1,0:T(8,128)(2,1)S(1)} fusion(bf16[64,1024]{1,0:T(8,128)(2,1)S(1)} %all_gather.18, bf16[3,1024,1024]{2,1,0:T(8,128)(2,1)} %param.11), kind=kOutput, calls=%fused_computation.67 | convolution fusion | flops 134283264 | bytes 2359296 | tf_op jit(solution)/shard_map/dot_general | solution.py:115
  118.2 0.9 reshape.205
  119.2 1.2 dynamic_update_slice.24
  120.6 1.8 %dynamic_update_slice.25 = bf16[512,1024]{0,1:T(8,128)(2,1)S(1)} dynamic-update-slice(bf16[512,1024]{0,1:T(8,128)(2,1)S(1)} %dynamic_update_slice.24, bf16[64,1024]{0,1:T(8,128)(2,1)S(1)} %copy.29, s32[]{:T(128)S(6)} %select_n.162, s32[]{:T(128)} %constant.189.clone.1) | dynamic-update-slice | bytes 262148 | tf_op jit(solution)/shard_map/dynamic_update_slice | solution.py:34
  122.6 2.0 %dynamic_update_slice.26 = bf16[512,1024]{0,1:T(8,128)(2,1)S(1)} dynamic-update-slice(bf16[512,1024]{0,1:T(8,128)(2,1)S(1)} %dynamic_update_slice.25, bf16[64,1024]{0,1:T(8,128)(2,1)S(1)} %copy.30, s32[]{:T(128)S(6)} %select_n.164, s32[]{:T(128)} %constant.189.clone.1) | dynamic-update-slice | bytes 262148 | tf_op jit(solution)/shard_map/dynamic_update_slice | solution.py:42
  124.8 1.0 dynamic_update_slice.27
  126.0 1.2 dynamic_update_slice.28
  127.4 2.0 %dynamic_update_slice.29 = bf16[512,1024]{0,1:T(8,128)(2,1)S(1)} dynamic-update-slice(bf16[512,1024]{0,1:T(8,128)(2,1)S(1)} %dynamic_update_slice.28, bf16[64,1024]{0,1:T(8,128)(2,1)S(1)} %copy.33, s32[]{:T(128)S(6)} %select_n.170, s32[]{:T(128)} %constant.189.clone.1) | dynamic-update-slice | bytes 262148 | tf_op jit(solution)/shard_map/dynamic_update_slice | solution.py:34
  129.6 2.0 %dynamic_update_slice.30 = bf16[512,1024]{0,1:T(8,128)(2,1)S(1)} dynamic-update-slice(bf16[512,1024]{0,1:T(8,128)(2,1)S(1)} %dynamic_update_slice.29, bf16[64,1024]{0,1:T(8,128)(2,1)S(1)} %copy.34, s32[]{:T(128)S(6)} %select_n.172, s32[]{:T(128)} %constant.189.clone.1) | dynamic-update-slice | bytes 262148 | tf_op jit(solution)/shard_map/dynamic_update_slice | solution.py:42
  131.8 1.2 dynamic_update_slice.31
  133.0 1.5 fusion.29
  134.5 0.7 fusion.30
  135.2 1.5 copy.37
  136.7 0.7 fusion.49
  137.6 0.2 convert_element_type.37
  137.8 0.8 bitcast_select_fusion
  138.6 6.0 %all-to-all-start = ((bf16[8,16,1024]{2,1,0:T(8,128)(2,1)}), bf16[8,16,1024]{2,1,0:T(8,128)(2,1)S(1)}, u32[]{:S(2)}, u32[]{:S(2)}) async-start(bf16[8,16,1024]{2,1,0:T(8,128)(2,1)} %bitcast_select_fusion), calls=%async_computation | async-start | bytes 524288 | tf_op jit(solution)/shard_map/all_to_all | solution.py:164
  144.6 8.2 %all-to-all-done = bf16[8,16,1024]{2,1,0:T(8,128)(2,1)S(1)} async-done(((bf16[8,16,1024]{2,1,0:T(8,128)(2,1)}), bf16[8,16,1024]{2,1,0:T(8,128)(2,1)S(1)}, u32[]{:S(2)}, u32[]{:S(2)}) %all-to-all-start) | async-done | bytes 262176 | tf_op jit(solution)/shard_map/all_to_all | solution.py:164
  152.8 0.7 constant_dynamic-slice_fusion
  (50 shorter events, 2.1 us)
Async XLA Ops:
  6.5 28.1 %copy-start = (bf16[256,512]{1,0:T(8,128)(2,1)S(1)}, bf16[256,512]{1,0:T(8,128)(2,1)}, u32[]{:S(2)}) copy-start(bf16[256,512]{1,0:T(8,128)(2,1)} %param.7) | copy-start | bytes 786436
  6.5 29.5 %copy-start.7 = (f32[2,512]{1,0:T(2,128)S(1)}, f32[2,512]{1,0:T(2,128)}, u32[]{:S(2)}) copy-start(f32[2,512]{1,0:T(2,128)} %param.10) | copy-start | bytes 12292
  6.5 29.5 %copy-start.6 = (f32[2,1024]{1,0:T(2,128)S(1)}, f32[2,1024]{1,0:T(2,128)}, u32[]{:S(2)}) copy-start(f32[2,1024]{1,0:T(2,128)} %param.8) | copy-start | bytes 24580
  6.5 39.5 %all-gather.5.cloned.1.call-start = ((), (), s32[]{:S(2)}) async-start(), calls=%async_computation.1 | async-start | bytes 3145728 | tf_op jit(solution)/shard_map/all_gather | solution.py:100
  36.0 33.1 %all-gather.7.cloned.1.call-start = ((), (), s32[]{:S(2)}) async-start(), calls=%async_computation.2 | async-start | bytes 3145728 | tf_op jit(solution)/shard_map/all_gather | solution.py:100
  46.0 2.2 %copy-start.2 = (f32[512,1024]{1,0:T(8,128)S(1)}, f32[512,1024]{1,0:T(8,128)}, u32[]{:S(2)}) copy-start(f32[512,1024]{1,0:T(8,128)} %all-gather.5.cloned.1.call-done) | copy-start | bytes 6291460
  48.2 5.3 %copy-start.5 = (bf16[2,3,1024,512]{3,2,1,0:T(8,128)(2,1)S(1)}, bf16[2,3,1024,512]{3,2,1,0:T(8,128)(2,1)}, u32[]{:S(2)}) copy-start(bf16[2,3,1024,512]{3,2,1,0:T(8,128)(2,1)} %param.9) | copy-start | bytes 18874372
  54.2 1.2 copy-start.1
  57.1 78.1 %all-gather.9.cloned.1.call-start = ((), (), s32[]{:S(2)}) async-start(), calls=%async_computation.3 | async-start | bytes 1179648 | tf_op jit(solution)/shard_map/all_gather | solution.py:141
  69.0 2.2 %copy-start.3 = (f32[512,1024]{1,0:T(8,128)S(1)}, f32[512,1024]{1,0:T(8,128)}, u32[]{:S(2)}) copy-start(f32[512,1024]{1,0:T(8,128)} %all-gather.7.cloned.1.call-done) | copy-start | bytes 6291460
  78.3 2.0 %copy-start.4 = (f32[512,512]{1,0:T(8,128)S(1)}, f32[512,512]{1,0:T(8,128)}, u32[]{:S(2)}) copy-start(f32[512,512]{1,0:T(8,128)} %fusion.34) | copy-start | bytes 3145732
  89.3 8.6 %collective-permute-start = (bf16[64,1024]{1,0:T(8,128)(2,1)S(1)}, bf16[64,1024]{1,0:T(8,128)(2,1)S(1)}, u32[]{:S(2)}, u32[]{:S(2)}) collective-permute-start(bf16[64,1024]{1,0:T(8,128)(2,1)S(1)} %fusion.42), channel_id=1, source_target_pairs={{0,2},{2,4},{4,6},{6,8},{8,10},{10,12},{12,14},{14,0},{1,3},{3,5},... | collective-permute-start | bytes 393224 | tf_op jit(solution)/shard_map/ppermute | solution.py:33
  91.1 8.7 %collective-permute-start.1 = (bf16[64,1024]{1,0:T(8,128)(2,1)S(1)}, bf16[64,1024]{1,0:T(8,128)(2,1)S(1)}, u32[]{:S(2)}, u32[]{:S(2)}) collective-permute-start(bf16[64,1024]{1,0:T(8,128)(2,1)S(1)} %fusion.42), channel_id=1, source_target_pairs={{0,14},{2,0},{4,2},{6,4},{8,6},{10,8},{12,10},{14,12},{1,15},{3,1}... | collective-permute-start | bytes 393224 | tf_op jit(solution)/shard_map/ppermute | solution.py:41
  98.0 10.2 %collective-permute-start.2 = (bf16[64,1024]{1,0:T(8,128)(2,1)S(1)}, bf16[64,1024]{1,0:T(8,128)(2,1)S(1)}, u32[]{:S(2)}, u32[]{:S(2)}) collective-permute-start(bf16[64,1024]{1,0:T(8,128)(2,1)S(1)} %collective-permute-done), channel_id=1, source_target_pairs={{0,2},{2,4},{4,6},{6,8},{8,10},{10,12},{12,14},{14,0},{1,3},{3,5},... | collective-permute-start | bytes 393224 | tf_op jit(solution)/shard_map/ppermute | solution.py:33
  99.8 8.5 %collective-permute-start.3 = (bf16[64,1024]{1,0:T(8,128)(2,1)S(1)}, bf16[64,1024]{1,0:T(8,128)(2,1)S(1)}, u32[]{:S(2)}, u32[]{:S(2)}) collective-permute-start(bf16[64,1024]{1,0:T(8,128)(2,1)S(1)} %collective-permute-done.1), channel_id=1, source_target_pairs={{0,14},{2,0},{4,2},{6,4},{8,6},{10,8},{12,10},{14,12},{1,15},{3,1}... | collective-permute-start | bytes 393224 | tf_op jit(solution)/shard_map/ppermute | solution.py:41
  108.2 7.8 %collective-permute-start.4 = (bf16[64,1024]{1,0:T(8,128)(2,1)S(1)}, bf16[64,1024]{1,0:T(8,128)(2,1)S(1)}, u32[]{:S(2)}, u32[]{:S(2)}) collective-permute-start(bf16[64,1024]{1,0:T(8,128)(2,1)S(1)} %collective-permute-done.2), channel_id=1, source_target_pairs={{0,2},{2,4},{4,6},{6,8},{8,10},{10,12},{12,14},{14,0},{1,3},{3,5},... | collective-permute-start | bytes 393224 | tf_op jit(solution)/shard_map/ppermute | solution.py:33
  108.3 21.1 %collective-permute-start.5 = (bf16[64,1024]{1,0:T(8,128)(2,1)S(1)}, bf16[64,1024]{1,0:T(8,128)(2,1)S(1)}, u32[]{:S(2)}, u32[]{:S(2)}) collective-permute-start(bf16[64,1024]{1,0:T(8,128)(2,1)S(1)} %collective-permute-done.3), channel_id=1, source_target_pairs={{0,14},{2,0},{4,2},{6,4},{8,6},{10,8},{12,10},{14,12},{1,15},{3,1}... | collective-permute-start | bytes 393224 | tf_op jit(solution)/shard_map/ppermute | solution.py:41
  116.0 15.7 %collective-permute-start.6 = (bf16[64,1024]{1,0:T(8,128)(2,1)S(1)}, bf16[64,1024]{1,0:T(8,128)(2,1)S(1)}, u32[]{:S(2)}, u32[]{:S(2)}) collective-permute-start(bf16[64,1024]{1,0:T(8,128)(2,1)S(1)} %collective-permute-done.4), channel_id=1, source_target_pairs={{0,2},{2,4},{4,6},{6,8},{8,10},{10,12},{12,14},{14,0},{1,3},{3,5},... | collective-permute-start | bytes 393224 | tf_op jit(solution)/shard_map/ppermute | solution.py:33
  138.6 14.2 %all-to-all-start = ((bf16[8,16,1024]{2,1,0:T(8,128)(2,1)}), bf16[8,16,1024]{2,1,0:T(8,128)(2,1)S(1)}, u32[]{:S(2)}, u32[]{:S(2)}) async-start(bf16[8,16,1024]{2,1,0:T(8,128)(2,1)} %bitcast_select_fusion), calls=%async_computation | async-start | bytes 524288 | tf_op jit(solution)/shard_map/all_to_all | solution.py:164
Sparse Core Ops, SparseCore 0:
  36.1 9.8 all-gather.4
  57.3 11.7 all-gather.6
  87.4 44.0 all-gather.8
